TPU v7x, 32 devices: a whole 2x2x4 slice. The times are simulated.
32 devices in a mesh: group: 2 (over y), visit: 16 (over z, x, core), sky: 1.
Axes of the slice: x: 2, y: 2, z: 4, core: 2. Of those that a mesh axis runs over, the one named last changes fastest.
Arguments:
- template: bfloat16 [64, 128], P(('group', 'visit'), 'sky'), parts along dimension 0, may hold values from -6 to 6
- science: float32 [32, 32, 128], P(('group', 'visit'), None, 'sky'), parts along dimension 0, may hold values from -15 to 15
- variance: float32 [32, 32, 128], P(('group', 'visit'), None, 'sky'), parts along dimension 0, may hold values from 0.5 to 4
- col_taps: bfloat16 [49, 31], replicated, may hold values from -1 to 1
- row_taps: bfloat16 [49, 31], replicated, may hold values from -1 to 1
- stamp_rows: int32 [32, 1, 16], P(('group', 'visit'), 'sky'), parts along dimension 0, may hold values from 0 to 16
- stamp_cols: int32 [32, 1, 16], P(('group', 'visit'), 'sky'), parts along dimension 0, may hold values from 0 to 112
Outputs:
- difference: float32 [32, 32, 128], P(('group', 'visit'), None, 'sky'), parts along dimension 0
- coefficients: float32 [32, 50], P(('group', 'visit')), parts along dimension 0
- detection: float32 [64, 128], P(('group', 'visit'), 'sky'), parts along dimension 0
There are 2 independent parts, one for each index of `group`. A program takes and returns all parts, laid end to end along the dimension named above; an argument that names none is the same for every part. Nothing has to cross between parts.
All inputs are finite; a program needn't handle non-finite values.
Results may differ from a plain program's by a relative error of at most 0.0018.
Values may be sent and summed in bfloat16 or wider, within the bound.
A program may use at most 128 MiB of HBM per device.

v0:
```python
import jax
import jax.numpy as jnp
from jax import lax
from jax.sharding import PartitionSpec as P

KBLK = 7
STAMP = 16


def with_halo(cells, sides, width):
    for axis, dim in sides:
        count = lax.axis_size(axis)
        ends = count - 1
        head = lax.slice_in_dim(cells, 0, width, axis=dim)
        tail = lax.slice_in_dim(cells, cells.shape[dim] - width, cells.shape[dim], axis=dim)
        cells = jnp.concatenate(
            [
                lax.ppermute(tail, axis, [(i, (i + 1) % count) for i in range(ends)]),
                cells,
                lax.ppermute(head, axis, [((i + 1) % count, i) for i in range(ends)]),
            ],
            axis=dim,
        )
    return cells


def tap_selectors(out_len, in_len, tap_count):
    offsets = (
        jnp.arange(in_len, dtype=jnp.int32)[None, :] - jnp.arange(out_len, dtype=jnp.int32)[:, None]
    )
    return (offsets[None, :, :] == jnp.arange(tap_count, dtype=jnp.int32)[:, None, None]).astype(
        jnp.float32
    )


def column_pass(padded, taps_block):
    tap_count = taps_block.shape[1]
    out_width = padded.shape[1] - tap_count + 1
    selectors = tap_selectors(out_width, padded.shape[1], tap_count)
    band_mats = jnp.einsum("kj,jci->kic", taps_block.astype(jnp.float32), selectors).astype(
        jnp.bfloat16
    )
    result = jnp.einsum("ri,kic->krc", padded, band_mats, preferred_element_type=jnp.float32)
    return result.astype(jnp.bfloat16)


def band_matrix(taps_block, out_len, in_len):
    tap_count = taps_block.shape[1]
    offsets = (
        jnp.arange(in_len, dtype=jnp.int32)[None, :] - jnp.arange(out_len, dtype=jnp.int32)[:, None]
    )
    taps_wide = taps_block.astype(jnp.float32)
    band = jnp.zeros((taps_block.shape[0], out_len, in_len), jnp.float32)
    for offset in range(tap_count):
        band = band + jnp.where(
            offsets[None, :, :] == offset, taps_wide[:, offset][:, None, None], 0.0
        )
    return band.astype(jnp.bfloat16)


def row_pass(columns, taps_block):
    tap_count = taps_block.shape[1]
    margin = (tap_count - 1) // 2
    height = columns.shape[1]
    stride = min(512, height)
    padded = jnp.pad(columns, ((0, 0), (margin, margin), (0, 0)))
    band = band_matrix(taps_block, stride, stride + 2 * margin)
    pieces = jnp.einsum("kti,kiw->ktw", band, padded, preferred_element_type=jnp.float32).astype(
        jnp.bfloat16
    )
    return pieces


def extract_stamps(block, row_starts, col_starts):

    def extract(row_start, col_start):
        return lax.dynamic_slice(
            block, (jnp.int32(0), row_start, col_start), (block.shape[0], STAMP, STAMP)
        )

    stamps = jax.vmap(extract)(row_starts, col_starts)
    return jnp.transpose(stamps, (1, 0, 2, 3)).reshape(block.shape[0], -1)


def extract_plane(plane, row_starts, col_starts):

    def extract(row_start, col_start):
        return lax.dynamic_slice(plane, (row_start, col_start), (STAMP, STAMP))

    return jax.vmap(extract)(row_starts, col_starts).reshape(-1)


def cholesky_solve(matrix, vector):
    factor = jnp.linalg.cholesky(matrix)
    middle = lax.linalg.triangular_solve(factor, vector[:, None], left_side=True, lower=True)
    answer = lax.linalg.triangular_solve(
        factor, middle, left_side=True, lower=True, transpose_a=True
    )
    return answer[:, 0]


def on_device(template, science, variance, col_taps, row_taps, stamp_rows, stamp_cols):
    tap_count = col_taps.shape[1]
    margin = (tap_count - 1) // 2
    kernels = col_taps.shape[0]
    blocks = kernels // KBLK
    science_map = science[0]
    variance_map = variance[0]
    inverse = 1.0 / variance_map
    gathered = lax.all_gather(template, "visit", axis=0, tiled=True)
    padded_tile = with_halo(gathered, (("sky", 1),), margin)
    image_list = []
    for block_index in range(blocks):
        image_list.append(
            row_pass(
                column_pass(padded_tile, col_taps[block_index * KBLK : (block_index + 1) * KBLK]),
                row_taps[block_index * KBLK : (block_index + 1) * KBLK],
            )
        )
    convolved = jnp.concatenate(image_list, axis=0)
    row_starts = stamp_rows[0, 0]
    col_starts = stamp_cols[0, 0]
    design_core = extract_stamps(convolved, row_starts, col_starts)
    design = jnp.concatenate(
        [design_core, jnp.ones((1, design_core.shape[1]), design_core.dtype)], axis=0
    ).astype(jnp.float32)
    weights = 1.0 / extract_plane(variance_map, row_starts, col_starts)
    values = extract_plane(science_map, row_starts, col_starts)
    partial_normal = jnp.dot(design * weights[None, :], design.T, precision=lax.Precision.HIGHEST)
    partial_target = jnp.dot(design, weights * values, precision=lax.Precision.HIGHEST)
    normal, target = lax.psum((partial_normal, partial_target), "sky")
    solution = cholesky_solve(normal, target)

    def model_step(block_index, total):
        images = lax.dynamic_slice_in_dim(convolved, block_index * KBLK, KBLK, 0).astype(
            jnp.float32
        )
        share = lax.dynamic_slice_in_dim(solution, block_index * KBLK, KBLK, 0)
        return total + jnp.tensordot(share, images, axes=1, precision=lax.Precision.HIGHEST)

    model_map = lax.fori_loop(0, blocks, model_step, jnp.zeros(science_map.shape, jnp.float32))
    residual = science_map - model_map - solution[kernels]
    difference = (residual / jnp.sqrt(variance_map))[None, :, :]
    weighted = residual / variance_map
    numerator, weight_total = (
        lax.psum_scatter(weighted, "visit", scatter_dimension=0, tiled=True),
        lax.psum_scatter(inverse, "visit", scatter_dimension=0, tiled=True),
    )
    detection = numerator / jnp.sqrt(weight_total)
    return (difference, solution[None, :], detection)


def solution(mesh):
    in_specs = (
        P(("group", "visit"), "sky"),
        P(("group", "visit"), None, "sky"),
        P(("group", "visit"), None, "sky"),
        P(),
        P(),
        P(("group", "visit"), "sky", None),
        P(("group", "visit"), "sky", None),
    )
    out_specs = (
        P(("group", "visit"), None, "sky"),
        P(("group", "visit"), None),
        P(("group", "visit"), "sky"),
    )
    return jax.shard_map(
        on_device, mesh=mesh, in_specs=in_specs, out_specs=out_specs, check_vma=False
    )
```

profile of v0, /device:TPU:0, one launch (start us, length us, event | category | flops | bytes accessed | tf_op | source)
XLA Modules:
  0.0 237.7 jit_solution(4948356048800179354)
XLA Ops:
  0.6 23.1 %all-gather = bf16[16,2,128]{2,1,0:T(2,128)(2,1)S(1)} all-gather(bf16[1,2,128]{2,1,0:T(2,128)(2,1)} %bitcast.593), channel_id=1, replica_groups=mesh['group'=2,'visit'=16,'sky'=1] {'visit'}, dimensions={0}, use_global_device_ids=true | all-gather | bytes 8704 | tf_op jit(solution)/shard_map/all_gather | solution.py:110
  26.6 1.7 fusion.34
  28.3 1.8 fusion.33
  30.1 1.7 fusion.32
  31.9 1.8 fusion.31
  33.7 1.8 fusion.30
  35.6 1.8 fusion.29
  37.4 1.9 fusion.28
  39.4 30.6 %while.18 = (s32[]{:T(128)}, f32[32,128]{1,0:T(8,128)S(1)}, s32[16,2]{0,1:T(2,128)S(1)}, f32[16,16,16]{2,1,0:T(8,128)S(1)}, s32[]{:T(128)}) while((s32[]{:T(128)}, f32[32,128]{1,0:T(8,128)S(1)}, s32[16,2]{0,1:T(2,128)S(1)}, f32[16,16,16]{2,1,0:T(8,128)S(1)}, s32[]{:T(128)}) %tuple.319), condition=%wide.while_cond.1, body=%wide.while_body.1.sunk | while | flops 2 | bytes 16493 | solution.py:88
  70.0 31.5 %while.19 = (s32[]{:T(128)}, f32[32,128]{1,0:T(8,128)S(1)}, s32[16,2]{0,1:T(2,128)S(1)}, f32[16,16,16]{2,1,0:T(8,128)S(1)}, s32[]{:T(128)}) while((s32[]{:T(128)}, f32[32,128]{1,0:T(8,128)S(1)}, s32[16,2]{0,1:T(2,128)S(1)}, f32[16,16,16]{2,1,0:T(8,128)S(1)}, s32[]{:T(128)}) %tuple.321), condition=%wide.while_cond.2, body=%wide.while_body.2.sunk | while | flops 2 | bytes 16493 | solution.py:88
  70.6 1.4 bitcast_dynamic-update-slice_fusion.8
  72.6 1.4 bitcast_dynamic-update-slice_fusion.8
  74.5 1.4 bitcast_dynamic-update-slice_fusion.8
  76.5 1.4 bitcast_dynamic-update-slice_fusion.8
  78.5 1.4 bitcast_dynamic-update-slice_fusion.8
  80.4 1.4 bitcast_dynamic-update-slice_fusion.8
  82.4 1.4 bitcast_dynamic-update-slice_fusion.8
  84.4 1.4 bitcast_dynamic-update-slice_fusion.8
  86.3 1.4 bitcast_dynamic-update-slice_fusion.8
  88.3 1.4 bitcast_dynamic-update-slice_fusion.8
  90.3 1.4 bitcast_dynamic-update-slice_fusion.8
  92.2 1.4 bitcast_dynamic-update-slice_fusion.8
  94.2 1.4 bitcast_dynamic-update-slice_fusion.8
  96.2 1.4 bitcast_dynamic-update-slice_fusion.8
  98.1 1.4 bitcast_dynamic-update-slice_fusion.8
  112.5 45.1 %while.17 = (s32[]{:T(128)}, bf16[49,32,128]{2,1,0:T(8,128)(2,1)S(1)}, s32[16,3]{0,1:T(4,128)S(1)}, bf16[16,49,16,16]{3,2,1,0:T(8,128)(2,1)}, s32[]{:T(128)}) while((s32[]{:T(128)}, bf16[49,32,128]{2,1,0:T(8,128)(2,1)S(1)}, s32[16,3]{0,1:T(4,128)S(1)}, bf16[16,49,16,16]{3,2,1,0:T(8,128)(2,1)}, s32[]{:T(128)}) %tuple.312), condition=%wide.while_cond, body=%wide.while_body.sunk | while | flops 2 | bytes 227433 | solution.py:77
  113.2 2.1 bitcast_dynamic-update-slice_fusion.6
  116.0 2.1 bitcast_dynamic-update-slice_fusion.6
  118.8 2.2 bitcast_dynamic-update-slice_fusion.6
  121.6 2.2 bitcast_dynamic-update-slice_fusion.6
  124.4 2.1 bitcast_dynamic-update-slice_fusion.6
  127.2 2.2 bitcast_dynamic-update-slice_fusion.6
  130.1 2.1 bitcast_dynamic-update-slice_fusion.6
  132.9 2.2 bitcast_dynamic-update-slice_fusion.6
  135.7 2.1 bitcast_dynamic-update-slice_fusion.6
  138.5 2.2 bitcast_dynamic-update-slice_fusion.6
  141.3 2.2 bitcast_dynamic-update-slice_fusion.6
  144.2 2.2 bitcast_dynamic-update-slice_fusion.6
  147.0 2.2 bitcast_dynamic-update-slice_fusion.6
  149.8 2.1 bitcast_dynamic-update-slice_fusion.6
  152.6 2.2 bitcast_dynamic-update-slice_fusion.6
  155.4 2.1 bitcast_dynamic-update-slice_fusion.6
  157.6 4.3 %copy.27 = bf16[49,16,16,16]{0,3,2,1:T(8,128)(2,1)S(1)} copy(bf16[49,16,16,16]{3,2,0,1:T(8,128)(2,1)} %bitcast.581) | data formatting | bytes 802816 | tf_op jit(solution)/shard_map/transpose | solution.py:82
  161.9 2.4 %fusion.11 = f32[50,50]{1,0:T(8,128)S(1)} fusion(f32[4096]{0:T(1024)S(1)} %div.38, bf16[49,4096]{0,1:T(8,128)(2,1)S(1)} %bitcast.579), kind=kOutput, calls=%fused_computation.20 | convolution fusion | flops 123289600 | bytes 427792 | tf_op jit(solution)/shard_map/dot_general | solution.py:129
  164.5 4.6 %cholesky.16 = f32[50,50]{1,0:T(8,128)S(1)} custom-call(f32[50,50]{1,0:T(8,128)S(1)} %fusion.511), custom_call_target="Cholesky" | custom-call | tf_op jit(solution)/shard_map/jit(cholesky)/cholesky | solution.py:94
  170.4 3.8 %custom-call.8 = f32[1,50,50]{1,2,0:T(8,128)S(1)} custom-call(f32[1,50,50]{2,1,0:T(8,128)S(1)} %fusion.507), custom_call_target="InvertDiagBlocksLowerTriangular" | custom-call | tf_op jit(solution)/shard_map/triangular_solve | solution.py:96
  175.7 2.3 while.20
  179.3 57.8 %all-reduce.10 = (f32[32,128]{1,0:T(8,128)S(1)}, f32[32,128]{1,0:T(8,128)S(1)}) all-reduce(f32[32,128]{1,0:T(8,128)S(1)} %get-tuple-element.164, f32[32,128]{1,0:T(8,128)S(1)} %get-tuple-element.162), channel_id=3, replica_groups=mesh['group'=2,'visit'=16,'sky'=1] {'visit'}, use_global_device_ids=true, to_apply=%region_5.6.clone | all-reduce | flops 8192 | bytes 65536
  (226 shorter events, 71.5 us)
Async XLA Ops:
  0.6 31.2 %copy-start.5 = (bf16[49,31]{0,1:T(8,128)(2,1)S(1)}, bf16[49,31]{0,1:T(8,128)(2,1)}, u32[]{:S(2)}) copy-start(bf16[49,31]{0,1:T(8,128)(2,1)} %param.12) | copy-start | bytes 9118
  23.9 79.1 %collective-permute-start = (bf16[32,15]{1,0:T(8,128)(2,1)S(1)}, bf16[32,15]{1,0:T(8,128)(2,1)S(1)}, u32[]{:S(2)}, u32[]{:S(2)}) collective-permute-start(bf16[32,15]{1,0:T(8,128)(2,1)S(1)} %get-tuple-element.389), channel_id=1, source_target_pairs={} | collective-permute-start | bytes 2888 | tf_op jit(solution)/shard_map/ppermute | solution.py:18
  24.5 78.5 %collective-permute-start.1 = (bf16[32,15]{1,0:T(8,128)(2,1)S(1)}, bf16[32,15]{1,0:T(8,128)(2,1)S(1)}, u32[]{:S(2)}, u32[]{:S(2)}) collective-permute-start(bf16[32,15]{1,0:T(8,128)(2,1)S(1)} %get-tuple-element.390), channel_id=1, source_target_pairs={} | collective-permute-start | bytes 2888 | tf_op jit(solution)/shard_map/ppermute | solution.py:20
  28.3 11.0 %copy-start.3 = (s32[1,1,16]{2,1,0:T(1,128)S(1)}, s32[1,1,16]{2,1,0:T(1,128)}, u32[]{:S(2)}) copy-start(s32[1,1,16]{2,1,0:T(1,128)} %param.15) | copy-start | bytes 196
  28.3 11.0 %copy-start.4 = (s32[1,1,16]{2,1,0:T(1,128)S(1)}, s32[1,1,16]{2,1,0:T(1,128)}, u32[]{:S(2)}) copy-start(s32[1,1,16]{2,1,0:T(1,128)} %param.14) | copy-start | bytes 196
  30.0 9.3 %copy-start = (f32[1,32,128]{2,1,0:T(8,128)S(1)}, f32[1,32,128]{2,1,0:T(8,128)}, u32[]{:S(2)}) copy-start(f32[1,32,128]{2,1,0:T(8,128)} %param.11) | copy-start | bytes 49156
  30.1 39.9 %copy-start.1 = (f32[1,32,128]{2,1,0:T(8,128)S(1)}, f32[1,32,128]{2,1,0:T(8,128)}, u32[]{:S(2)}) copy-start(f32[1,32,128]{2,1,0:T(8,128)} %param.10) | copy-start | bytes 49156
  31.8 69.9 %copy-start.6 = (u32[32]{0:T(128)S(1)}, u32[32]{0:T(128)}, u32[]{:S(2)}) copy-start(u32[32]{0:T(128)} %constant.223) | copy-start | bytes 388
  103.0 4.8 %copy-start.7 = (bf16[7,158,128]{1,0,2:T(8,128)(2,1)S(1)}, bf16[7,158,128]{1,0,2:T(8,128)(2,1)}, u32[]{:S(2)}) copy-start(bf16[7,158,128]{1,0,2:T(8,128)(2,1)} %fusion.28) | copy-start | bytes 849412
  178.0 59.6 %copy-start.2 = (f32[50]{0:T(128)}, f32[50]{0:T(128)S(1)}, u32[]{:S(2)}) copy-start(f32[50]{0:T(128)S(1)} %get-tuple-element.611) | copy-start | bytes 604
where the time goes:
time: 239 us; the launch traced here: 238 us
  local copies, waits for them, and re-layouts  113 us (47%)
  blocking collectives  80.9 us (34%)
  matrix products  27 us (11%)
  other arithmetic  13 us (5%)
    gather x144, local copies, waits for them, and re-layouts  107 us
    unnamed x1, blocking collectives  57.8 us
    all_gather x1, blocking collectives, on_device(): gathered = lax.all_gather(template, 'visit', axis=0, tiled=True)  23.1 us
    dot_general x7, matrix products, column_pass(): jnp.einsum('kj,jci->kic', taps_block.astype(jnp.float32), selectors)  12.6 us
    another operation x3, other arithmetic, cholesky_solve(): factor = jnp.linalg.cholesky(matrix)  5.24 us
    dot_general x7, matrix products, column_pass(): jnp.einsum('ri,kic->krc', padded, band_mats, preferred_element_type=jnp.f...  4.89 us
  transfers between devices with their start and end apart: 2, of which 0 were waited for; matrix products, arithmetic and copies ran while one was open for 32% of the time, Pallas kernels for 0%

commit v1 on v0

--- a/solution.py
+++ b/solution.py
@@ -1,6 +1,10 @@
+import functools
+
 import jax
 import jax.numpy as jnp
 from jax import lax
+from jax.experimental import pallas as pl
+from jax.experimental.pallas import tpu as pltpu
 from jax.sharding import PartitionSpec as P
 
 KBLK = 7
@@ -150,6 +154,281 @@
     return (difference, solution[None, :], detection)
 
 
+MESH = pl.DeviceIdType.MESH
+SUB = 8
+EXTRA = 4
+
+
+def dot(a, b, contract=((1,), (0,))):
+    return lax.dot_general(a, b, (contract, ((), ())), preferred_element_type=jnp.float32)
+
+
+def split3(value):
+    high = value.astype(jnp.bfloat16)
+    rest = value - high.astype(jnp.float32)
+    middle = rest.astype(jnp.bfloat16)
+    low = (rest - middle.astype(jnp.float32)).astype(jnp.bfloat16)
+    return high, middle, low
+
+
+def iota(shape, dim):
+    return lax.broadcasted_iota(jnp.int32, shape, dim)
+
+
+def placed_taps(taps, lanes, sign):
+    count = taps.shape[1]
+    margin = (count - 1) // 2
+    spot = sign * (iota((count, lanes), 0) - margin)
+    spot = jnp.where(spot < 0, spot + lanes, spot)
+    place = jnp.where(iota((count, lanes), 1) == spot, 1.0, 0.0).astype(jnp.bfloat16)
+    return dot(taps, place)
+
+
+def fused_kernel(
+    n,
+    template_ref,
+    science_ref,
+    variance_ref,
+    col_taps_ref,
+    row_taps_ref,
+    stamp_rows_ref,
+    stamp_cols_ref,
+    difference_ref,
+    coefficients_ref,
+    detection_ref,
+    outbox,
+    inbox,
+    parts_out,
+    parts_in,
+    tile,
+    col_bands,
+    row_bands,
+    design,
+    send_a,
+    recv_a,
+    send_b,
+    recv_b,
+):
+    me = lax.axis_index("visit")
+    kernels, taps = col_taps_ref.shape
+    margin = (taps - 1) // 2
+    share, width = template_ref.shape
+    height = science_ref.shape[1]
+    groups = row_bands.shape[0]
+    stacked = SUB * height
+
+    def copies(source, target, send, recv):
+        return [
+            pltpu.make_async_remote_copy(
+                src_ref=source.at[lax.rem(me + step, n)],
+                dst_ref=target.at[me],
+                send_sem=send.at[step],
+                recv_sem=recv.at[step],
+                device_id={"visit": lax.rem(me + step, n)},
+                device_id_type=MESH,
+            )
+            for step in range(1, n)
+        ]
+
+    barrier = pltpu.get_barrier_semaphore()
+    for step in range(1, n):
+        pl.semaphore_signal(
+            barrier, inc=1, device_id={"visit": lax.rem(me + step, n)}, device_id_type=MESH
+        )
+
+    science = science_ref[0]
+    variance = variance_ref[0]
+    inverse = 1.0 / variance
+    own_rows = template_ref[...].astype(jnp.float32)
+    for owner in range(n):
+        outbox[owner, 0:share, :] = own_rows
+        outbox[owner, share : 2 * share, :] = inverse[owner * share : (owner + 1) * share]
+    inbox[me] = outbox[me]
+
+    spread = placed_taps(row_taps_ref[...], stacked, 1)
+    spread = jnp.concatenate(
+        [spread, jnp.zeros((groups * SUB - kernels, stacked), jnp.float32)], axis=0
+    )
+    own_block = iota((SUB, stacked), 1) // height == iota((SUB, stacked), 0)
+    for group in range(groups):
+        source = spread[group * SUB : (group + 1) * SUB]
+        base = source
+        for sub in range(1, SUB):
+            base = jnp.where(
+                iota((SUB, stacked), 0) == sub, pltpu.roll(source, sub * height, 1), base
+            )
+        for row in range(0, height, 2):
+            pair = [
+                jnp.where(own_block, pltpu.roll(base, row + more, 1), 0.0) for more in range(2)
+            ]
+            row_bands[group, row * SUB : (row + 2) * SUB, :] = jnp.concatenate(
+                pair, axis=0
+            ).astype(jnp.bfloat16)
+
+    pl.semaphore_wait(barrier, n - 1)
+    first = copies(outbox, inbox, send_a, recv_a)
+    for copy in first:
+        copy.start()
+
+    lanes = placed_taps(col_taps_ref[...], width, -1)
+    near = jnp.abs(iota((width, width), 0) - iota((width, width), 1)) <= margin
+    for k in range(kernels):
+        base = pltpu.roll(
+            jnp.broadcast_to(lanes[k : k + 1], (width, width)), 0, 1, stride=1, stride_axis=0
+        )
+        col_bands[:, k * width : (k + 1) * width] = jnp.where(near, base, 0.0).astype(jnp.bfloat16)
+
+    tops = stamp_rows_ref[0]
+    lefts = stamp_cols_ref[0]
+    down = iota((height, tops.shape[1]), 0) - tops
+    across = iota((width, lefts.shape[1]), 0) - lefts
+    in_rows = jnp.where((down >= 0) & (down < STAMP), 1.0, 0.0).astype(jnp.bfloat16)
+    in_cols = jnp.where((across >= 0) & (across < STAMP), 1.0, 0.0).astype(jnp.bfloat16)
+    weights = dot(in_rows, in_cols, ((1,), (1,))) * inverse
+    pieces = [p.astype(jnp.float32) for p in split3(science)]
+
+    def constant_rows(group, row):
+        block = jnp.zeros((SUB, width), jnp.float32)
+        for extra in range(EXTRA):
+            index = kernels + extra - group * SUB
+            if 0 <= index < SUB:
+                entry = (
+                    jnp.ones((1, width), jnp.float32)
+                    if extra == 0
+                    else pieces[extra - 1][row : row + 1]
+                )
+                block = jnp.where(iota((SUB, width), 0) == index, entry, block)
+        return block
+
+    for copy in first:
+        copy.wait_recv()
+    for owner in range(n):
+        tile[owner * share : (owner + 1) * share, :] = inbox[owner, 0:share, :]
+    weight_total = inbox[0, share : 2 * share, :]
+    for owner in range(1, n):
+        weight_total = weight_total + inbox[owner, share : 2 * share, :]
+    scale = jnp.sqrt(weight_total)
+
+    columns = dot(tile[...].astype(jnp.bfloat16), col_bands[...]).astype(jnp.bfloat16)
+    for group in range(groups):
+        members = range(group * SUB, min((group + 1) * SUB, kernels))
+        if len(members):
+            block = jnp.concatenate([columns[:, k * width : (k + 1) * width] for k in members], 0)
+            images = dot(row_bands[group, :, 0 : len(members) * height], block)
+            images = images.astype(jnp.bfloat16).astype(jnp.float32)
+        else:
+            images = jnp.zeros((stacked, width), jnp.float32)
+        for row in range(height):
+            image = images[row * SUB : (row + 1) * SUB]
+            if (group + 1) * SUB > kernels:
+                image = image + constant_rows(group, row)
+            design[row, group * SUB : (group + 1) * SUB, :] = image
+
+    flat = jnp.concatenate([design[row] for row in range(height)], axis=1)
+    flat_weights = jnp.concatenate([weights[row : row + 1] for row in range(height)], axis=1)
+    gap = jnp.zeros((-flat.shape[0] % 16, flat.shape[1]), jnp.float32)
+    flat = jnp.concatenate([flat, gap], axis=0)
+    left = jnp.concatenate(split3(flat * flat_weights), axis=0)
+    grams = dot(left, flat.astype(jnp.bfloat16), ((1,), (1,)))
+    size = flat.shape[0]
+    gram = grams[0:size] + grams[size : 2 * size] + grams[2 * size : 3 * size]
+    gram = gram[0 : groups * SUB]
+    unknowns = kernels + 1
+    target = gram[:, unknowns : unknowns + 1]
+    for extra in range(2, EXTRA):
+        target = target + gram[:, kernels + extra : kernels + extra + 1]
+    gram = jnp.where(iota(gram.shape, 1) == unknowns, target, gram)
+
+    system = [gram[g * SUB : (g + 1) * SUB] for g in range(groups)]
+    lanes_wide = system[0].shape[1]
+    subs = iota((SUB, lanes_wide), 0)
+    scales = [jnp.zeros((SUB, lanes_wide), jnp.float32) for _ in range(groups)]
+    for k in range(unknowns):
+        home, sub = divmod(k, SUB)
+        row = jnp.broadcast_to(system[home][sub : sub + 1], (SUB, lanes_wide))
+        pivot = 1.0 / jnp.broadcast_to(row[:, k : k + 1], (SUB, lanes_wide))
+        scaled = row * pivot
+        scales[home] = jnp.where(subs == sub, pivot, scales[home])
+        for g in range(groups):
+            factor = jnp.broadcast_to(system[g][:, k : k + 1], (SUB, lanes_wide))
+            if g == home:
+                factor = jnp.where(subs == sub, 0.0, factor)
+            system[g] = system[g] - factor * scaled
+    answers = [
+        jnp.broadcast_to(system[g][:, unknowns : unknowns + 1] * scales[g][:, 0:1], (SUB, width))
+        for g in range(groups)
+    ]
+    answer = jnp.concatenate(answers, axis=0)
+
+    model = jnp.sum(design[...] * answer[None], axis=1)
+    residual = science - model
+    weighted = residual * inverse
+    for owner in range(n):
+        parts_out[owner] = weighted[owner * share : (owner + 1) * share]
+    parts_in[me] = parts_out[me]
+    second = copies(parts_out, parts_in, send_b, recv_b)
+    for copy in second:
+        copy.start()
+
+    difference_ref[0] = residual / jnp.sqrt(variance)
+    across = jnp.sum(
+        jnp.where(iota(answer.shape, 0) == iota(answer.shape, 1), answer, 0.0), axis=0, keepdims=True
+    )
+    coefficients_ref[...] = across[:, 0:unknowns]
+
+    for copy in second:
+        copy.wait_recv()
+    numerator = parts_in[0]
+    for owner in range(1, n):
+        numerator = numerator + parts_in[owner]
+    detection_ref[...] = numerator / scale
+    for copy in first + second:
+        copy.wait_send()
+
+
+def fused(n, template, science, variance, col_taps, row_taps, stamp_rows, stamp_cols):
+    kernels = col_taps.shape[0]
+    share, width = template.shape
+    height = science.shape[1]
+    groups = -(-(kernels + EXTRA) // SUB)
+    stacked = SUB * height
+    vmem = pl.BlockSpec(memory_space=pltpu.VMEM)
+    return pl.pallas_call(
+        functools.partial(fused_kernel, n),
+        out_shape=(
+            jax.ShapeDtypeStruct(science.shape, jnp.float32),
+            jax.ShapeDtypeStruct((1, kernels + 1), jnp.float32),
+            jax.ShapeDtypeStruct((share, width), jnp.float32),
+        ),
+        in_specs=[vmem] * 7,
+        out_specs=(vmem,) * 3,
+        scratch_shapes=[
+            pltpu.VMEM((n, 2 * share, width), jnp.float32),
+            pltpu.VMEM((n, 2 * share, width), jnp.float32),
+            pltpu.VMEM((n, share, width), jnp.float32),
+            pltpu.VMEM((n, share, width), jnp.float32),
+            pltpu.VMEM((height, width), jnp.float32),
+            pltpu.VMEM((width, kernels * width), jnp.bfloat16),
+            pltpu.VMEM((groups, stacked, stacked), jnp.bfloat16),
+            pltpu.VMEM((height, groups * SUB, width), jnp.float32),
+            pltpu.SemaphoreType.DMA((n,)),
+            pltpu.SemaphoreType.DMA((n,)),
+            pltpu.SemaphoreType.DMA((n,)),
+            pltpu.SemaphoreType.DMA((n,)),
+        ],
+        compiler_params=pltpu.CompilerParams(
+            collective_id=0, has_side_effects=True, vmem_limit_bytes=32 * 2**20
+        ),
+    )(template, science, variance, col_taps, row_taps, stamp_rows, stamp_cols)
+
+
+def per_device(axes, template, science, *rest):
+    height, width = science.shape[1:]
+    if axes["sky"] == 1 and width % 128 == 0 and SUB * height <= 2 * width:
+        return fused(axes["visit"], template, science, *rest)
+    return on_device(template, science, *rest)
+
+
 def solution(mesh):
     in_specs = (
         P(("group", "visit"), "sky"),
@@ -166,5 +445,5 @@
         P(("group", "visit"), "sky"),
     )
     return jax.shard_map(
-        on_device, mesh=mesh, in_specs=in_specs, out_specs=out_specs, check_vma=False
-    )
+        functools.partial(per_device, dict(mesh.shape)), mesh=mesh, in_specs=in_specs, out_specs=out_specs, check_vma=False
+    )

time: 239 us -> 27.5 us (0.12)
  local copies, waits for them, and re-layouts: 113 us -> 3.2 us
  blocking collectives: 80.9 us -> 0 us
  matrix products: 27 us -> 0 us
  Pallas kernels: 0 us -> 23.2 us
  other arithmetic: 13 us -> 0 us
    gather x144 -> x0, local copies, waits for them, and re-layouts: 107 us -> none
    unnamed x1 -> x0, blocking collectives: 57.8 us -> none
    dot_general x30 -> x0, matrix products: 26.7 us -> none  [the longest x7 12.6 us: column_pass(): jnp.einsum('kj,jci->kic', taps_block.astype(jnp.float32), selectors)]
    pallas_call x0 -> x1, Pallas kernels: none -> 23.2 us  [fused(): pl.pallas_call(functools.partial(fused_kernel, n), out_shape=(jax.ShapeDt...]
    all_gather x1 -> x0, blocking collectives: 23.1 us -> none  [on_device(): gathered = lax.all_gather(template, 'visit', axis=0, tiled=True)]
    another operation x5 -> x0, other arithmetic: 9.72 us -> none  [the longest x3 5.24 us: cholesky_solve(): factor = jnp.linalg.cholesky(matrix)]
    transpose x1 -> x0, local copies, waits for them, and re-layouts: 4.33 us -> none  [extract_stamps(): return jnp.transpose(stamps, (1, 0, 2, 3)).reshape(block.shape[0], -1)]
    unnamed x19 -> x17, local copies, waits for them, and re-layouts: 0.65 us -> 3.2 us
  transfers between devices with their start and end apart: 2 -> 0, of which waited for: 0 -> 0; matrix products, arithmetic and copies ran while one was open for 32% -> 0% of each run, Pallas kernels for 0% -> 0%
where the time goes in v1:
time: 27.5 us; the launch traced here: 27.1 us
  Pallas kernels  23.2 us (84%)
  local copies, waits for them, and re-layouts  3.2 us (12%)
  between operations  0.69 us (3%)
    pallas_call x1, Pallas kernels, fused(): pl.pallas_call(functools.partial(fused_kernel, n), out_shape=(jax.ShapeDt...  23.2 us
    unnamed x17, local copies, waits for them, and re-layouts  3.2 us

profile of v1, /device:TPU:0, one launch (start us, length us, event | category | flops | bytes accessed | tf_op | source)
XLA Modules:
  0.0 27.1 jit_solution(4672876123355617566)
XLA Ops:
  0.6 0.0 copy-start.5
  0.6 0.0 copy-start.1
  0.7 0.8 %copy.10.col_taps_ref = bf16[49,31]{1,0:T(8,128)(2,1)S(1)} copy(bf16[49,31]{0,1:T(8,128)(2,1)} %param.10) | data formatting | bytes 6076 | tf_op args[3]
  1.5 0.0 copy-done.5
  1.5 0.0 copy-start
  1.5 0.0 copy-start.2
  1.5 0.0 copy-start.3
  1.5 0.0 copy-start.4
  1.5 0.1 copy.11.row_taps_ref
  1.6 0.0 copy-done.1
  1.6 0.6 %copy-done = f32[1,32,128]{2,1,0:T(8,128)S(1)} copy-done((f32[1,32,128]{2,1,0:T(8,128)S(1)}, f32[1,32,128]{2,1,0:T(8,128)}, u32[]{:S(2)}) %copy-start) | copy-done | bytes 16408
  2.2 0.0 copy-done.2
  2.2 0.0 copy-done.3
  2.2 0.0 copy-done.4
  2.2 23.2 %shard_map.94 = (f32[1,32,128]{2,1,0:T(8,128)S(1)}, f32[1,50]{1,0:T(1,128)S(1)}, f32[2,128]{1,0:T(2,128)S(1)}) custom-call(bf16[2,128]{1,0:T(2,128)(2,1)S(1)} %copy-done.2, f32[1,32,128]{2,1,0:T(8,128)S(1)} %copy-done, f32[1,32,128]{2,1,0:T(8,128)S(1)} %copy-done.1, bf16[49,31]{1,0:T(8,128)(2,1)S(1)} %copy.10.col_taps_ref, ...), custom_call_target="tpu_custom_call" | custom-call | tf_op jit(solution)/shard_map/pallas_call | solution.py:396
  25.5 0.6 %copy.15 = f32[1,32,128]{2,1,0:T(8,128)} copy(f32[1,32,128]{2,1,0:T(8,128)S(1)} %get-tuple-element.6) | data formatting | bytes 32768
  26.1 0.5 %copy.16 = f32[1,50]{1,0:T(1,128)} copy(f32[1,50]{1,0:T(1,128)S(1)} %get-tuple-element.7) | data formatting | bytes 400
  26.6 0.6 %copy.17 = f32[2,128]{1,0:T(2,128)} copy(f32[2,128]{1,0:T(2,128)S(1)} %get-tuple-element.8) | data formatting | bytes 2048
Async XLA Ops:
  0.6 0.8 %copy-start.5 = (bf16[49,31]{0,1:T(8,128)(2,1)S(1)}, bf16[49,31]{0,1:T(8,128)(2,1)}, u32[]{:S(2)}) copy-start(bf16[49,31]{0,1:T(8,128)(2,1)} %param.11) | copy-start | bytes 9118
  0.6 1.0 %copy-start.1 = (f32[1,32,128]{2,1,0:T(8,128)S(1)}, f32[1,32,128]{2,1,0:T(8,128)}, u32[]{:S(2)}) copy-start(f32[1,32,128]{2,1,0:T(8,128)} %variance_ref.1) | copy-start | bytes 49156
  1.5 0.7 %copy-start = (f32[1,32,128]{2,1,0:T(8,128)S(1)}, f32[1,32,128]{2,1,0:T(8,128)}, u32[]{:S(2)}) copy-start(f32[1,32,128]{2,1,0:T(8,128)} %science_ref.1) | copy-start | bytes 49156
  1.5 0.7 %copy-start.2 = (bf16[2,128]{1,0:T(2,128)(2,1)S(1)}, bf16[2,128]{1,0:T(2,128)(2,1)}, u32[]{:S(2)}) copy-start(bf16[2,128]{1,0:T(2,128)(2,1)} %template_ref.1) | copy-start | bytes 1540
  1.5 0.7 %copy-start.3 = (s32[1,1,16]{2,1,0:T(1,128)S(1)}, s32[1,1,16]{2,1,0:T(1,128)}, u32[]{:S(2)}) copy-start(s32[1,1,16]{2,1,0:T(1,128)} %stamp_rows_ref.1) | copy-start | bytes 196
  1.5 0.7 %copy-start.4 = (s32[1,1,16]{2,1,0:T(1,128)S(1)}, s32[1,1,16]{2,1,0:T(1,128)}, u32[]{:S(2)}) copy-start(s32[1,1,16]{2,1,0:T(1,128)} %stamp_cols_ref.1) | copy-start | bytes 196

commit v2 on v1

--- a/solution.py
+++ b/solution.py
@@ -156,6 +156,9 @@
 
 MESH = pl.DeviceIdType.MESH
 SUB = 8
+OPERANDS = 7
+RESULTS = 3
+VMEM_BYTES = 60 * 2**20
 EXTRA = 4
 
 
@@ -176,23 +179,35 @@
 
 
 def placed_taps(taps, lanes, sign):
-    count = taps.shape[1]
+    count = taps.shape[0]
     margin = (count - 1) // 2
     spot = sign * (iota((count, lanes), 0) - margin)
     spot = jnp.where(spot < 0, spot + lanes, spot)
     place = jnp.where(iota((count, lanes), 1) == spot, 1.0, 0.0).astype(jnp.bfloat16)
-    return dot(taps, place)
+    return dot(taps, place, ((0,), (0,)))
 
 
 def fused_kernel(
     n,
-    template_ref,
-    science_ref,
-    variance_ref,
-    col_taps_ref,
-    row_taps_ref,
-    stamp_rows_ref,
-    stamp_cols_ref,
+    *refs,
+):
+    operands, refs = refs[:OPERANDS], refs[OPERANDS:]
+    results, refs = refs[:RESULTS], refs[RESULTS:]
+    held, loaded, refs = refs[:OPERANDS], refs[OPERANDS], refs[OPERANDS + 1 :]
+    ready, stored, refs = refs[:RESULTS], refs[RESULTS], refs[RESULTS + 1 :]
+    stores = [
+        pltpu.make_async_copy(here, result, stored.at[i])
+        for i, (here, result) in enumerate(zip(ready, results))
+    ]
+    body(n, operands, held, loaded, stores, *ready, *refs)
+
+
+def body(
+    n,
+    operands,
+    held,
+    loaded,
+    stores,
     difference_ref,
     coefficients_ref,
     detection_ref,
@@ -209,8 +224,10 @@
     send_b,
     recv_b,
 ):
+    template_ref, science_ref, variance_ref, col_taps_ref, row_taps_ref = held[:5]
+    stamp_rows_ref, stamp_cols_ref = held[5:]
     me = lax.axis_index("visit")
-    kernels, taps = col_taps_ref.shape
+    taps, kernels = col_taps_ref.shape
     margin = (taps - 1) // 2
     share, width = template_ref.shape
     height = science_ref.shape[1]
@@ -236,6 +253,15 @@
             barrier, inc=1, device_id={"visit": lax.rem(me + step, n)}, device_id_type=MESH
         )
 
+    fetches = [
+        pltpu.make_async_copy(operand, here, loaded.at[i])
+        for i, (operand, here) in enumerate(zip(operands, held))
+    ]
+    for fetch in fetches:
+        fetch.start()
+    for fetch in fetches:
+        fetch.wait()
+
     science = science_ref[0]
     variance = variance_ref[0]
     inverse = 1.0 / variance
@@ -245,25 +271,25 @@
         outbox[owner, share : 2 * share, :] = inverse[owner * share : (owner + 1) * share]
     inbox[me] = outbox[me]
 
-    spread = placed_taps(row_taps_ref[...], stacked, 1)
+    spread = placed_taps(row_taps_ref[...], width, 1)
     spread = jnp.concatenate(
-        [spread, jnp.zeros((groups * SUB - kernels, stacked), jnp.float32)], axis=0
-    )
-    own_block = iota((SUB, stacked), 1) // height == iota((SUB, stacked), 0)
+        [spread, jnp.zeros((groups * SUB - kernels, width), jnp.float32)], axis=0
+    )
+    per_tile = width // height
+    sub_of = iota((SUB, width), 0)
     for group in range(groups):
         source = spread[group * SUB : (group + 1) * SUB]
         base = source
-        for sub in range(1, SUB):
-            base = jnp.where(
-                iota((SUB, stacked), 0) == sub, pltpu.roll(source, sub * height, 1), base
-            )
+        for slot in range(1, per_tile):
+            base = jnp.where(sub_of % per_tile == slot, pltpu.roll(source, slot * height, 1), base)
         for row in range(0, height, 2):
-            pair = [
-                jnp.where(own_block, pltpu.roll(base, row + more, 1), 0.0) for more in range(2)
-            ]
-            row_bands[group, row * SUB : (row + 2) * SUB, :] = jnp.concatenate(
-                pair, axis=0
-            ).astype(jnp.bfloat16)
+            turned = [pltpu.roll(base, row + more, 1) for more in range(2)]
+            for part in range(stacked // width):
+                own = iota((SUB, width), 1) // height + part * per_tile == sub_of
+                pair = [jnp.where(own, one, 0.0) for one in turned]
+                row_bands[
+                    group, row * SUB : (row + 2) * SUB, part * width : (part + 1) * width
+                ] = jnp.concatenate(pair, axis=0).astype(jnp.bfloat16)
 
     pl.semaphore_wait(barrier, n - 1)
     first = copies(outbox, inbox, send_a, recv_a)
@@ -340,22 +366,49 @@
     gram = jnp.where(iota(gram.shape, 1) == unknowns, target, gram)
 
     system = [gram[g * SUB : (g + 1) * SUB] for g in range(groups)]
-    lanes_wide = system[0].shape[1]
-    subs = iota((SUB, lanes_wide), 0)
-    scales = [jnp.zeros((SUB, lanes_wide), jnp.float32) for _ in range(groups)]
-    for k in range(unknowns):
-        home, sub = divmod(k, SUB)
-        row = jnp.broadcast_to(system[home][sub : sub + 1], (SUB, lanes_wide))
-        pivot = 1.0 / jnp.broadcast_to(row[:, k : k + 1], (SUB, lanes_wide))
-        scaled = row * pivot
-        scales[home] = jnp.where(subs == sub, pivot, scales[home])
+    shape = system[0].shape
+    subs = iota(shape, 0)
+    for home in range(groups):
+        begin = home * SUB
+        size = min(SUB, unknowns - begin)
+        if size <= 0:
+            break
+        factors = [
+            [jnp.broadcast_to(part[:, begin + s : begin + s + 1], shape) for s in range(size)]
+            for part in system
+        ]
+        rows = [jnp.broadcast_to(system[home][s : s + 1], shape) for s in range(size)]
+        pivots = [
+            [jnp.broadcast_to(factors[home][s][t : t + 1], shape) for s in range(size)]
+            for t in range(size)
+        ]
+        for s in range(size):
+            scale_by = 1.0 / pivots[s][s]
+            for u in range(s + 1, size):
+                pivots[s][u] = pivots[s][u] * scale_by
+            rows[s] = rows[s] * scale_by
+            for t in range(size):
+                if t == s:
+                    continue
+                by = pivots[t][s]
+                for u in range(s + 1, size):
+                    pivots[t][u] = pivots[t][u] - by * pivots[s][u]
+                rows[t] = rows[t] - by * rows[s]
         for g in range(groups):
-            factor = jnp.broadcast_to(system[g][:, k : k + 1], (SUB, lanes_wide))
             if g == home:
-                factor = jnp.where(subs == sub, 0.0, factor)
-            system[g] = system[g] - factor * scaled
+                for s in range(size):
+                    system[g] = jnp.where(subs == s, rows[s], system[g])
+                continue
+            change = factors[g][0] * rows[0]
+            for s in range(1, size):
+                change = change + factors[g][s] * rows[s]
+            system[g] = system[g] - change
     answers = [
-        jnp.broadcast_to(system[g][:, unknowns : unknowns + 1] * scales[g][:, 0:1], (SUB, width))
+        jnp.where(
+            iota((SUB, width), 0) + g * SUB < unknowns,
+            jnp.broadcast_to(system[g][:, unknowns : unknowns + 1], (SUB, width)),
+            0.0,
+        )
         for g in range(groups)
     ]
     answer = jnp.concatenate(answers, axis=0)
@@ -375,6 +428,8 @@
         jnp.where(iota(answer.shape, 0) == iota(answer.shape, 1), answer, 0.0), axis=0, keepdims=True
     )
     coefficients_ref[...] = across[:, 0:unknowns]
+    for store in stores[:-1]:
+        store.start()
 
     for copy in second:
         copy.wait_recv()
@@ -382,8 +437,22 @@
     for owner in range(1, n):
         numerator = numerator + parts_in[owner]
     detection_ref[...] = numerator / scale
+    stores[-1].start()
     for copy in first + second:
         copy.wait_send()
+    for store in stores:
+        store.wait()
+
+
+def hand_over(*refs):
+    done = refs[-1]
+    moves = [
+        pltpu.make_async_copy(refs[i], refs[RESULTS + i], done.at[i]) for i in range(RESULTS)
+    ]
+    for move in moves:
+        move.start()
+    for move in moves:
+        move.wait()
 
 
 def fused(n, template, science, variance, col_taps, row_taps, stamp_rows, stamp_cols):
@@ -392,17 +461,25 @@
     height = science.shape[1]
     groups = -(-(kernels + EXTRA) // SUB)
     stacked = SUB * height
-    vmem = pl.BlockSpec(memory_space=pltpu.VMEM)
-    return pl.pallas_call(
+    hbm = pl.BlockSpec(memory_space=pltpu.HBM)
+    operands = (template, science, variance, col_taps.T, row_taps.T, stamp_rows, stamp_cols)
+    shapes = (
+        jax.ShapeDtypeStruct(science.shape, jnp.float32),
+        jax.ShapeDtypeStruct((1, kernels + 1), jnp.float32),
+        jax.ShapeDtypeStruct((share, width), jnp.float32),
+    )
+    results = pl.pallas_call(
         functools.partial(fused_kernel, n),
-        out_shape=(
-            jax.ShapeDtypeStruct(science.shape, jnp.float32),
-            jax.ShapeDtypeStruct((1, kernels + 1), jnp.float32),
-            jax.ShapeDtypeStruct((share, width), jnp.float32),
-        ),
-        in_specs=[vmem] * 7,
-        out_specs=(vmem,) * 3,
-        scratch_shapes=[
+        out_shape=shapes,
+        in_specs=[hbm] * OPERANDS,
+        out_specs=(hbm,) * RESULTS,
+        scratch_shapes=[pltpu.VMEM(operand.shape, operand.dtype) for operand in operands]
+        + [
+            pltpu.SemaphoreType.DMA((OPERANDS,)),
+        ]
+        + [pltpu.VMEM(shape.shape, shape.dtype) for shape in shapes]
+        + [
+            pltpu.SemaphoreType.DMA((RESULTS,)),
             pltpu.VMEM((n, 2 * share, width), jnp.float32),
             pltpu.VMEM((n, 2 * share, width), jnp.float32),
             pltpu.VMEM((n, share, width), jnp.float32),
@@ -417,14 +494,22 @@
             pltpu.SemaphoreType.DMA((n,)),
         ],
         compiler_params=pltpu.CompilerParams(
-            collective_id=0, has_side_effects=True, vmem_limit_bytes=32 * 2**20
+            collective_id=0, has_side_effects=True, vmem_limit_bytes=VMEM_BYTES
         ),
-    )(template, science, variance, col_taps, row_taps, stamp_rows, stamp_cols)
+    )(*operands)
+    return pl.pallas_call(
+        hand_over,
+        out_shape=shapes,
+        in_specs=[hbm] * RESULTS,
+        out_specs=(hbm,) * RESULTS,
+        scratch_shapes=[pltpu.SemaphoreType.DMA((RESULTS,))],
+        compiler_params=pltpu.CompilerParams(vmem_limit_bytes=VMEM_BYTES),
+    )(*results)
 
 
 def per_device(axes, template, science, *rest):
     height, width = science.shape[1:]
-    if axes["sky"] == 1 and width % 128 == 0 and SUB * height <= 2 * width:
+    if axes["sky"] == 1 and width % 128 == 0 and SUB * height == 2 * width:
         return fused(axes["visit"], template, science, *rest)
     return on_device(template, science, *rest)
 

time: 27.5 us -> 21.7 us (0.79)
  local copies, waits for them, and re-layouts: 3.2 us -> 0 us
  Pallas kernels: 23.2 us -> 20.9 us
    unnamed x17 -> x0, local copies, waits for them, and re-layouts: 3.2 us -> none
    pallas_call x1 -> x2, Pallas kernels: 23.2 us -> 20.9 us  [the longest x1 19.2 us: fused(): pl.pallas_call(functools.partial(fused_kernel, n), out_shape=shapes, in_s...]
where the time goes in v2:
time: 21.7 us; the launch traced here: 21.5 us
  Pallas kernels  20.9 us (96%)
  between operations  0.64 us (3%)
    pallas_call x1, Pallas kernels, fused(): pl.pallas_call(functools.partial(fused_kernel, n), out_shape=shapes, in_s...  19.2 us
    pallas_call x1, Pallas kernels, fused(): pl.pallas_call(hand_over, out_shape=shapes, in_specs=[hbm] * RESULTS, out...  1.67 us

profile of v2, /device:TPU:0, one launch (start us, length us, event | category | flops | bytes accessed | tf_op | source)
XLA Modules:
  0.0 21.5 jit_solution(9288698173538832530)
XLA Ops:
  0.6 19.2 %shard_map.94 = (f32[1,32,128]{2,1,0:T(8,128)}, f32[1,50]{1,0:T(1,128)}, f32[2,128]{1,0:T(2,128)}) custom-call(bf16[2,128]{1,0:T(2,128)(2,1)} %refs_0_.1, f32[1,32,128]{2,1,0:T(8,128)} %refs_1_.1, f32[1,32,128]{2,1,0:T(8,128)} %refs_2_.1, bf16[31,49]{1,0:T(8,128)(2,1)} %bitcast.2, bf16[31,49]{1,0:T(8,128)(2,1)} %bitcast.3, s32[1,1,16]{2,1,0:T(1,128)} %refs_5_.1, ...), custom_call_target="tpu_custom_call" | custom-call | tf_op jit(solution)/shard_map/pallas_call | solution.py:471
  19.9 1.7 %shard_map.95 = (f32[1,32,128]{2,1,0:T(8,128)}, f32[1,50]{1,0:T(1,128)}, f32[2,128]{1,0:T(2,128)}) custom-call(f32[1,32,128]{2,1,0:T(8,128)} %get-tuple-element.6.refs_0_, f32[1,50]{1,0:T(1,128)} %get-tuple-element.7.refs_1_, f32[2,128]{1,0:T(2,128)} %get-tuple-element.8.refs_2_), custom_call_target="tpu_custom_call" | custom-call | tf_op jit(solution)/shard_map/pallas_call | solution.py:500

commit v3 on v2

--- a/solution.py
+++ b/solution.py
@@ -178,13 +178,21 @@
     return lax.broadcasted_iota(jnp.int32, shape, dim)
 
 
-def placed_taps(taps, lanes, sign):
+def placed_taps(taps, lanes, spot, block):
     count = taps.shape[0]
-    margin = (count - 1) // 2
-    spot = sign * (iota((count, lanes), 0) - margin)
-    spot = jnp.where(spot < 0, spot + lanes, spot)
-    place = jnp.where(iota((count, lanes), 1) == spot, 1.0, 0.0).astype(jnp.bfloat16)
-    return dot(taps, place, ((0,), (0,)))
+    here = iota((count, lanes), 1) // block == spot(iota((count, lanes), 0))
+    return dot(taps, jnp.where(here, 1.0, 0.0).astype(jnp.bfloat16), ((0,), (0,)))
+
+
+def padded_rows(value, rows):
+    gap = jnp.zeros((rows - value.shape[0], value.shape[1]), value.dtype)
+    return jnp.concatenate([value, gap], axis=0)
+
+
+def reciprocal(value):
+    guess = pl.reciprocal(value, approx=True)
+    guess = guess * (2.0 - value * guess)
+    return guess * (2.0 - value * guess)
 
 
 def fused_kernel(
@@ -216,7 +224,6 @@
     parts_out,
     parts_in,
     tile,
-    col_bands,
     row_bands,
     design,
     send_a,
@@ -259,7 +266,7 @@
     ]
     for fetch in fetches:
         fetch.start()
-    for fetch in fetches:
+    for fetch in fetches[:3]:
         fetch.wait()
 
     science = science_ref[0]
@@ -271,38 +278,43 @@
         outbox[owner, share : 2 * share, :] = inverse[owner * share : (owner + 1) * share]
     inbox[me] = outbox[me]
 
-    spread = placed_taps(row_taps_ref[...], width, 1)
-    spread = jnp.concatenate(
-        [spread, jnp.zeros((groups * SUB - kernels, width), jnp.float32)], axis=0
-    )
-    per_tile = width // height
-    sub_of = iota((SUB, width), 0)
+    for fetch in fetches[3:]:
+        fetch.wait()
+
+    spread = placed_taps(
+        row_taps_ref[...],
+        stacked,
+        lambda j: jnp.where(j < margin, j - margin + height, j - margin),
+        SUB,
+    )
+    spread = padded_rows(spread, groups * SUB)
+    own = iota((SUB, stacked), 1) % SUB == iota((SUB, stacked), 0)
+    lane_row = iota((SUB, stacked), 1) // SUB
     for group in range(groups):
-        source = spread[group * SUB : (group + 1) * SUB]
-        base = source
-        for slot in range(1, per_tile):
-            base = jnp.where(sub_of % per_tile == slot, pltpu.roll(source, slot * height, 1), base)
+        base = jnp.where(own, spread[group * SUB : (group + 1) * SUB], 0.0)
         for row in range(0, height, 2):
-            turned = [pltpu.roll(base, row + more, 1) for more in range(2)]
-            for part in range(stacked // width):
-                own = iota((SUB, width), 1) // height + part * per_tile == sub_of
-                pair = [jnp.where(own, one, 0.0) for one in turned]
-                row_bands[
-                    group, row * SUB : (row + 2) * SUB, part * width : (part + 1) * width
-                ] = jnp.concatenate(pair, axis=0).astype(jnp.bfloat16)
+            pair = [
+                jnp.where(
+                    jnp.abs(lane_row - (row + more)) <= margin,
+                    pltpu.roll(base, SUB * (row + more), 1) if row + more else base,
+                    0.0,
+                )
+                for more in range(2)
+            ]
+            row_bands[group, row * SUB : (row + 2) * SUB, :] = jnp.concatenate(
+                pair, axis=0
+            ).astype(jnp.bfloat16)
 
     pl.semaphore_wait(barrier, n - 1)
     first = copies(outbox, inbox, send_a, recv_a)
     for copy in first:
         copy.start()
 
-    lanes = placed_taps(col_taps_ref[...], width, -1)
-    near = jnp.abs(iota((width, width), 0) - iota((width, width), 1)) <= margin
-    for k in range(kernels):
-        base = pltpu.roll(
-            jnp.broadcast_to(lanes[k : k + 1], (width, width)), 0, 1, stride=1, stride_axis=0
-        )
-        col_bands[:, k * width : (k + 1) * width] = jnp.where(near, base, 0.0).astype(jnp.bfloat16)
+    depth = -(-taps // 16) * 16
+    col_taps = placed_taps(col_taps_ref[...], depth, lambda j: taps - 1 - j, 1)
+    col_taps = padded_rows(col_taps, -(-groups * SUB // 16) * 16).astype(jnp.bfloat16)
+    source_col = iota((depth, width), 1) + margin - iota((depth, width), 0)
+    inside = (source_col >= 0) & (source_col < width)
 
     tops = stamp_rows_ref[0]
     lefts = stamp_cols_ref[0]
@@ -335,15 +347,30 @@
         weight_total = weight_total + inbox[owner, share : 2 * share, :]
     scale = jnp.sqrt(weight_total)
 
-    columns = dot(tile[...].astype(jnp.bfloat16), col_bands[...]).astype(jnp.bfloat16)
+    shifted = [
+        jnp.where(
+            inside,
+            pltpu.roll(
+                jnp.broadcast_to(tile[row : row + 1, :], (depth, width)),
+                width - margin,
+                1,
+                stride=1,
+                stride_axis=0,
+            ),
+            0.0,
+        ).astype(jnp.bfloat16)
+        for row in range(height)
+    ]
+    columns = dot(col_taps, jnp.concatenate(shifted, axis=1))
     for group in range(groups):
-        members = range(group * SUB, min((group + 1) * SUB, kernels))
-        if len(members):
-            block = jnp.concatenate([columns[:, k * width : (k + 1) * width] for k in members], 0)
-            images = dot(row_bands[group, :, 0 : len(members) * height], block)
-            images = images.astype(jnp.bfloat16).astype(jnp.float32)
-        else:
-            images = jnp.zeros((stacked, width), jnp.float32)
+        block = jnp.concatenate(
+            [
+                columns[group * SUB : (group + 1) * SUB, row * width : (row + 1) * width]
+                for row in range(height)
+            ],
+            axis=0,
+        ).astype(jnp.bfloat16)
+        images = dot(row_bands[group], block).astype(jnp.bfloat16).astype(jnp.float32)
         for row in range(height):
             image = images[row * SUB : (row + 1) * SUB]
             if (group + 1) * SUB > kernels:
@@ -383,7 +410,7 @@
             for t in range(size)
         ]
         for s in range(size):
-            scale_by = 1.0 / pivots[s][s]
+            scale_by = reciprocal(pivots[s][s])
             for u in range(s + 1, size):
                 pivots[s][u] = pivots[s][u] * scale_by
             rows[s] = rows[s] * scale_by
@@ -485,7 +512,6 @@
             pltpu.VMEM((n, share, width), jnp.float32),
             pltpu.VMEM((n, share, width), jnp.float32),
             pltpu.VMEM((height, width), jnp.float32),
-            pltpu.VMEM((width, kernels * width), jnp.bfloat16),
             pltpu.VMEM((groups, stacked, stacked), jnp.bfloat16),
             pltpu.VMEM((height, groups * SUB, width), jnp.float32),
             pltpu.SemaphoreType.DMA((n,)),
@@ -509,7 +535,7 @@
 
 def per_device(axes, template, science, *rest):
     height, width = science.shape[1:]
-    if axes["sky"] == 1 and width % 128 == 0 and SUB * height == 2 * width:
+    if axes["sky"] == 1 and width % 128 == 0 and SUB * height == 2 * width and rest[1].shape[1] <= height:
         return fused(axes["visit"], template, science, *rest)
     return on_device(template, science, *rest)
 

time: 21.7 us -> 22.3 us (1.028)
  Pallas kernels: 20.9 us -> 21.5 us
    pallas_call x1, Pallas kernels: 19.2 us -> 19.8 us  [fused(): pl.pallas_call(functools.partial(fused_kernel, n), out_shape=shapes, in_s...]
where the time goes in v3:
time: 22.3 us; the launch traced here: 22.1 us
  Pallas kernels  21.5 us (96%)
  between operations  0.64 us (3%)
    pallas_call x1, Pallas kernels, fused(): pl.pallas_call(functools.partial(fused_kernel, n), out_shape=shapes, in_s...  19.8 us
    pallas_call x1, Pallas kernels, fused(): pl.pallas_call(hand_over, out_shape=shapes, in_specs=[hbm] * RESULTS, out...  1.67 us

profile of v3, /device:TPU:0, one launch (start us, length us, event | category | flops | bytes accessed | tf_op | source)
XLA Modules:
  0.0 22.1 jit_solution(18182745081191740235)
XLA Ops:
  0.6 19.8 %shard_map.94 = (f32[1,32,128]{2,1,0:T(8,128)}, f32[1,50]{1,0:T(1,128)}, f32[2,128]{1,0:T(2,128)}) custom-call(bf16[2,128]{1,0:T(2,128)(2,1)} %refs_0_.1, f32[1,32,128]{2,1,0:T(8,128)} %refs_1_.1, f32[1,32,128]{2,1,0:T(8,128)} %refs_2_.1, bf16[31,49]{1,0:T(8,128)(2,1)} %bitcast.2, bf16[31,49]{1,0:T(8,128)(2,1)} %bitcast.3, s32[1,1,16]{2,1,0:T(1,128)} %refs_5_.1, ...), custom_call_target="tpu_custom_call" | custom-call | tf_op jit(solution)/shard_map/pallas_call | solution.py:498
  20.5 1.7 %shard_map.95 = (f32[1,32,128]{2,1,0:T(8,128)}, f32[1,50]{1,0:T(1,128)}, f32[2,128]{1,0:T(2,128)}) custom-call(f32[1,32,128]{2,1,0:T(8,128)} %get-tuple-element.6.refs_0_, f32[1,50]{1,0:T(1,128)} %get-tuple-element.7.refs_1_, f32[2,128]{1,0:T(2,128)} %get-tuple-element.8.refs_2_), custom_call_target="tpu_custom_call" | custom-call | tf_op jit(solution)/shard_map/pallas_call | solution.py:526

commit v4 on v2

--- a/solution.py
+++ b/solution.py
@@ -185,6 +185,12 @@
     spot = jnp.where(spot < 0, spot + lanes, spot)
     place = jnp.where(iota((count, lanes), 1) == spot, 1.0, 0.0).astype(jnp.bfloat16)
     return dot(taps, place, ((0,), (0,)))
+
+
+def reciprocal(value):
+    guess = pl.reciprocal(value, approx=True)
+    guess = guess * (2.0 - value * guess)
+    return guess * (2.0 - value * guess)
 
 
 def fused_kernel(
@@ -259,7 +265,7 @@
     ]
     for fetch in fetches:
         fetch.start()
-    for fetch in fetches:
+    for fetch in fetches[:3]:
         fetch.wait()
 
     science = science_ref[0]
@@ -270,6 +276,9 @@
         outbox[owner, 0:share, :] = own_rows
         outbox[owner, share : 2 * share, :] = inverse[owner * share : (owner + 1) * share]
     inbox[me] = outbox[me]
+
+    for fetch in fetches[3:]:
+        fetch.wait()
 
     spread = placed_taps(row_taps_ref[...], width, 1)
     spread = jnp.concatenate(
@@ -365,44 +374,72 @@
         target = target + gram[:, kernels + extra : kernels + extra + 1]
     gram = jnp.where(iota(gram.shape, 1) == unknowns, target, gram)
 
-    system = [gram[g * SUB : (g + 1) * SUB] for g in range(groups)]
-    shape = system[0].shape
+    parts = [gram[g * SUB : (g + 1) * SUB] for g in range(groups)]
+    shape = parts[0].shape
     subs = iota(shape, 0)
+    lane = iota(shape, 1)
+    on_diagonal = [(lane == subs + g * SUB) & (lane < unknowns) for g in range(groups)]
+    diagonals = [jnp.where(on_diagonal[g], parts[g], 0.0) for g in range(groups)]
+    along = jnp.sum(functools.reduce(jnp.add, diagonals), axis=0, keepdims=True)
+    along = lax.rsqrt(jnp.where(iota(along.shape, 1) < unknowns, along, 1.0))
+    down_scales = []
+    for g in range(groups):
+        entry = jnp.sum(diagonals[g], axis=1, keepdims=True)
+        entry = jnp.where(iota(entry.shape, 0) + g * SUB < unknowns, entry, 1.0)
+        down_scales.append(lax.rsqrt(jnp.broadcast_to(entry, shape)))
+    system = [parts[g] * along * down_scales[g] for g in range(groups)]
     for home in range(groups):
         begin = home * SUB
         size = min(SUB, unknowns - begin)
         if size <= 0:
             break
-        factors = [
-            [jnp.broadcast_to(part[:, begin + s : begin + s + 1], shape) for s in range(size)]
-            for part in system
+        rows = [jnp.broadcast_to(system[home][s : s + 1], shape) for s in range(size)]
+        own_factors = [
+            jnp.broadcast_to(system[home][:, begin + s : begin + s + 1], shape)
+            for s in range(size)
         ]
-        rows = [jnp.broadcast_to(system[home][s : s + 1], shape) for s in range(size)]
-        pivots = [
-            [jnp.broadcast_to(factors[home][s][t : t + 1], shape) for s in range(size)]
+        upper = {
+            (t, u): jnp.broadcast_to(own_factors[u][t : t + 1], shape)
             for t in range(size)
-        ]
-        for s in range(size):
-            scale_by = 1.0 / pivots[s][s]
-            for u in range(s + 1, size):
-                pivots[s][u] = pivots[s][u] * scale_by
-            rows[s] = rows[s] * scale_by
-            for t in range(size):
-                if t == s:
-                    continue
-                by = pivots[t][s]
-                for u in range(s + 1, size):
-                    pivots[t][u] = pivots[t][u] - by * pivots[s][u]
-                rows[t] = rows[t] - by * rows[s]
+            for u in range(t, size)
+        }
+        steps = []
+        for s in range(0, size, 2):
+            later = range(s + 2, size)
+            if s + 1 < size:
+                a, b, c = upper[s, s], upper[s, s + 1], upper[s + 1, s + 1]
+                det = reciprocal(a * c - b * b)
+                aa, bb, cc = c * det, -b * det, a * det
+                first_by = {u: aa * upper[s, u] + bb * upper[s + 1, u] for u in later}
+                second_by = {u: bb * upper[s, u] + cc * upper[s + 1, u] for u in later}
+                for t in later:
+                    for u in range(t, size):
+                        upper[t, u] = upper[t, u] - (
+                            upper[s, t] * first_by[u] + upper[s + 1, t] * second_by[u]
+                        )
+                rows[s], rows[s + 1] = (
+                    aa * rows[s] + bb * rows[s + 1],
+                    bb * rows[s] + cc * rows[s + 1],
+                )
+                for t in later:
+                    rows[t] = rows[t] - (upper[s, t] * rows[s] + upper[s + 1, t] * rows[s + 1])
+                steps += [(s, first_by), (s + 1, second_by)]
+            else:
+                rows[s] = rows[s] * reciprocal(upper[s, s])
+        for s, by in reversed(steps):
+            for u, value in by.items():
+                rows[s] = rows[s] - value * rows[u]
         for g in range(groups):
             if g == home:
                 for s in range(size):
                     system[g] = jnp.where(subs == s, rows[s], system[g])
                 continue
-            change = factors[g][0] * rows[0]
-            for s in range(1, size):
-                change = change + factors[g][s] * rows[s]
+            change = None
+            for s in range(size):
+                factor = jnp.broadcast_to(system[g][:, begin + s : begin + s + 1], shape)
+                change = factor * rows[s] if change is None else change + factor * rows[s]
             system[g] = system[g] - change
+    system = [system[g] * down_scales[g] for g in range(groups)]
     answers = [
         jnp.where(
             iota((SUB, width), 0) + g * SUB < unknowns,

time: 21.7 us -> 22 us (1.014)
    pallas_call x1, Pallas kernels: 19.2 us -> 19.5 us  [fused(): pl.pallas_call(functools.partial(fused_kernel, n), out_shape=shapes, in_s...]
where the time goes in v4:
time: 22 us; the launch traced here: 21.8 us
  Pallas kernels  21.1 us (96%)
  between operations  0.64 us (3%)
    pallas_call x1, Pallas kernels, fused(): pl.pallas_call(functools.partial(fused_kernel, n), out_shape=shapes, in_s...  19.5 us
    pallas_call x1, Pallas kernels, fused(): pl.pallas_call(hand_over, out_shape=shapes, in_specs=[hbm] * RESULTS, out...  1.67 us

profile of v4, /device:TPU:0, one launch (start us, length us, event | category | flops | bytes accessed | tf_op | source)
XLA Modules:
  0.0 21.8 jit_solution(6583616743987042212)
XLA Ops:
  0.6 19.5 %shard_map.94 = (f32[1,32,128]{2,1,0:T(8,128)}, f32[1,50]{1,0:T(1,128)}, f32[2,128]{1,0:T(2,128)}) custom-call(bf16[2,128]{1,0:T(2,128)(2,1)} %refs_0_.1, f32[1,32,128]{2,1,0:T(8,128)} %refs_1_.1, f32[1,32,128]{2,1,0:T(8,128)} %refs_2_.1, bf16[31,49]{1,0:T(8,128)(2,1)} %bitcast.2, bf16[31,49]{1,0:T(8,128)(2,1)} %bitcast.3, s32[1,1,16]{2,1,0:T(1,128)} %refs_5_.1, ...), custom_call_target="tpu_custom_call" | custom-call | tf_op jit(solution)/shard_map/pallas_call | solution.py:508
  20.1 1.7 %shard_map.95 = (f32[1,32,128]{2,1,0:T(8,128)}, f32[1,50]{1,0:T(1,128)}, f32[2,128]{1,0:T(2,128)}) custom-call(f32[1,32,128]{2,1,0:T(8,128)} %get-tuple-element.6.refs_0_, f32[1,50]{1,0:T(1,128)} %get-tuple-element.7.refs_1_, f32[2,128]{1,0:T(2,128)} %get-tuple-element.8.refs_2_), custom_call_target="tpu_custom_call" | custom-call | tf_op jit(solution)/shard_map/pallas_call | solution.py:537

commit v5 on v2

--- a/solution.py
+++ b/solution.py
@@ -156,9 +156,8 @@
 
 MESH = pl.DeviceIdType.MESH
 SUB = 8
-OPERANDS = 7
 RESULTS = 3
-VMEM_BYTES = 60 * 2**20
+VMEM_BYTES = 16 * 2**20
 EXTRA = 4
 
 
@@ -179,35 +178,23 @@
 
 
 def placed_taps(taps, lanes, sign):
-    count = taps.shape[0]
+    count = taps.shape[1]
     margin = (count - 1) // 2
     spot = sign * (iota((count, lanes), 0) - margin)
     spot = jnp.where(spot < 0, spot + lanes, spot)
     place = jnp.where(iota((count, lanes), 1) == spot, 1.0, 0.0).astype(jnp.bfloat16)
-    return dot(taps, place, ((0,), (0,)))
+    return dot(taps, place)
 
 
 def fused_kernel(
     n,
-    *refs,
-):
-    operands, refs = refs[:OPERANDS], refs[OPERANDS:]
-    results, refs = refs[:RESULTS], refs[RESULTS:]
-    held, loaded, refs = refs[:OPERANDS], refs[OPERANDS], refs[OPERANDS + 1 :]
-    ready, stored, refs = refs[:RESULTS], refs[RESULTS], refs[RESULTS + 1 :]
-    stores = [
-        pltpu.make_async_copy(here, result, stored.at[i])
-        for i, (here, result) in enumerate(zip(ready, results))
-    ]
-    body(n, operands, held, loaded, stores, *ready, *refs)
-
-
-def body(
-    n,
-    operands,
-    held,
-    loaded,
-    stores,
+    template_ref,
+    science_ref,
+    variance_ref,
+    col_taps_ref,
+    row_taps_ref,
+    stamp_rows_ref,
+    stamp_cols_ref,
     difference_ref,
     coefficients_ref,
     detection_ref,
@@ -224,10 +211,8 @@
     send_b,
     recv_b,
 ):
-    template_ref, science_ref, variance_ref, col_taps_ref, row_taps_ref = held[:5]
-    stamp_rows_ref, stamp_cols_ref = held[5:]
     me = lax.axis_index("visit")
-    taps, kernels = col_taps_ref.shape
+    kernels, taps = col_taps_ref.shape
     margin = (taps - 1) // 2
     share, width = template_ref.shape
     height = science_ref.shape[1]
@@ -252,15 +237,6 @@
         pl.semaphore_signal(
             barrier, inc=1, device_id={"visit": lax.rem(me + step, n)}, device_id_type=MESH
         )
-
-    fetches = [
-        pltpu.make_async_copy(operand, here, loaded.at[i])
-        for i, (operand, here) in enumerate(zip(operands, held))
-    ]
-    for fetch in fetches:
-        fetch.start()
-    for fetch in fetches:
-        fetch.wait()
 
     science = science_ref[0]
     variance = variance_ref[0]
@@ -428,8 +404,6 @@
         jnp.where(iota(answer.shape, 0) == iota(answer.shape, 1), answer, 0.0), axis=0, keepdims=True
     )
     coefficients_ref[...] = across[:, 0:unknowns]
-    for store in stores[:-1]:
-        store.start()
 
     for copy in second:
         copy.wait_recv()
@@ -437,11 +411,8 @@
     for owner in range(1, n):
         numerator = numerator + parts_in[owner]
     detection_ref[...] = numerator / scale
-    stores[-1].start()
     for copy in first + second:
         copy.wait_send()
-    for store in stores:
-        store.wait()
 
 
 def hand_over(*refs):
@@ -461,8 +432,9 @@
     height = science.shape[1]
     groups = -(-(kernels + EXTRA) // SUB)
     stacked = SUB * height
+    vmem = pl.BlockSpec(memory_space=pltpu.VMEM)
     hbm = pl.BlockSpec(memory_space=pltpu.HBM)
-    operands = (template, science, variance, col_taps.T, row_taps.T, stamp_rows, stamp_cols)
+    operands = (template, science, variance, col_taps, row_taps, stamp_rows, stamp_cols)
     shapes = (
         jax.ShapeDtypeStruct(science.shape, jnp.float32),
         jax.ShapeDtypeStruct((1, kernels + 1), jnp.float32),
@@ -471,15 +443,9 @@
     results = pl.pallas_call(
         functools.partial(fused_kernel, n),
         out_shape=shapes,
-        in_specs=[hbm] * OPERANDS,
-        out_specs=(hbm,) * RESULTS,
-        scratch_shapes=[pltpu.VMEM(operand.shape, operand.dtype) for operand in operands]
-        + [
-            pltpu.SemaphoreType.DMA((OPERANDS,)),
-        ]
-        + [pltpu.VMEM(shape.shape, shape.dtype) for shape in shapes]
-        + [
-            pltpu.SemaphoreType.DMA((RESULTS,)),
+        in_specs=[vmem] * len(operands),
+        out_specs=(vmem,) * RESULTS,
+        scratch_shapes=[
             pltpu.VMEM((n, 2 * share, width), jnp.float32),
             pltpu.VMEM((n, 2 * share, width), jnp.float32),
             pltpu.VMEM((n, share, width), jnp.float32),
@@ -500,7 +466,7 @@
     return pl.pallas_call(
         hand_over,
         out_shape=shapes,
-        in_specs=[hbm] * RESULTS,
+        in_specs=[vmem] * RESULTS,
         out_specs=(hbm,) * RESULTS,
         scratch_shapes=[pltpu.SemaphoreType.DMA((RESULTS,))],
         compiler_params=pltpu.CompilerParams(vmem_limit_bytes=VMEM_BYTES),

time: 21.7 us -> 21.8 us (level)
  Pallas kernels: 20.9 us -> 19.3 us
  local copies, waits for them, and re-layouts: 0 us -> 1.52 us
    unnamed x0 -> x14, local copies, waits for them, and re-layouts: none -> 1.52 us
    pallas_call x1, Pallas kernels: 1.67 us -> 0.64 us  [fused(): pl.pallas_call(hand_over, out_shape=shapes, in_specs=[vmem] * RESULTS, ou...]
    pallas_call x1, Pallas kernels: 19.2 us -> 18.6 us  [fused(): pl.pallas_call(functools.partial(fused_kernel, n), out_shape=shapes, in_s...]
where the time goes in v5:
time: 21.8 us; the launch traced here: 21.5 us
  Pallas kernels  19.3 us (89%)
  local copies, waits for them, and re-layouts  1.52 us (7%)
  between operations  0.69 us (3%)
    pallas_call x1, Pallas kernels, fused(): pl.pallas_call(functools.partial(fused_kernel, n), out_shape=shapes, in_s...  18.6 us
    unnamed x14, local copies, waits for them, and re-layouts  1.52 us
    pallas_call x1, Pallas kernels, fused(): pl.pallas_call(hand_over, out_shape=shapes, in_specs=[vmem] * RESULTS, ou...  0.64 us

profile of v5, /device:TPU:0, one launch (start us, length us, event | category | flops | bytes accessed | tf_op | source)
XLA Modules:
  0.0 21.5 jit_solution(13209230347574051674)
XLA Ops:
  0.6 0.0 copy-start.5
  0.6 0.0 copy-start.1
  0.7 0.8 %copy.10.col_taps_ref = bf16[49,31]{1,0:T(8,128)(2,1)S(1)} copy(bf16[49,31]{0,1:T(8,128)(2,1)} %param.10) | data formatting | bytes 6076 | tf_op args[3]
  1.5 0.0 copy-done.5
  1.5 0.0 copy-start
  1.5 0.0 copy-start.2
  1.5 0.0 copy-start.3
  1.5 0.0 copy-start.4
  1.5 0.1 copy.11.row_taps_ref
  1.6 0.0 copy-done.1
  1.6 0.6 %copy-done = f32[1,32,128]{2,1,0:T(8,128)S(1)} copy-done((f32[1,32,128]{2,1,0:T(8,128)S(1)}, f32[1,32,128]{2,1,0:T(8,128)}, u32[]{:S(2)}) %copy-start) | copy-done | bytes 16408
  2.2 0.0 copy-done.2
  2.2 0.0 copy-done.3
  2.2 0.0 copy-done.4
  2.2 18.6 %shard_map.94 = (f32[1,32,128]{2,1,0:T(8,128)S(1)}, f32[1,50]{1,0:T(1,128)S(1)}, f32[2,128]{1,0:T(2,128)S(1)}) custom-call(bf16[2,128]{1,0:T(2,128)(2,1)S(1)} %copy-done.2, f32[1,32,128]{2,1,0:T(8,128)S(1)} %copy-done, f32[1,32,128]{2,1,0:T(8,128)S(1)} %copy-done.1, bf16[49,31]{1,0:T(8,128)(2,1)S(1)} %copy.10.col_taps_ref, ...), custom_call_target="tpu_custom_call" | custom-call | tf_op jit(solution)/shard_map/pallas_call | solution.py:443
  20.8 0.6 %shard_map.95 = (f32[1,32,128]{2,1,0:T(8,128)}, f32[1,50]{1,0:T(1,128)}, f32[2,128]{1,0:T(2,128)}) custom-call(f32[1,32,128]{2,1,0:T(8,128)S(1)} %get-tuple-element.6.refs_0_, f32[1,50]{1,0:T(1,128)S(1)} %get-tuple-element.7.refs_1_, f32[2,128]{1,0:T(2,128)S(1)} %get-tuple-element.8.refs_2_), custom_call_target="tpu_custom_call" | custom-call | tf_op jit(solution)/shard_map/pallas_call | solution.py:466
Async XLA Ops:
  0.6 0.8 %copy-start.5 = (bf16[49,31]{0,1:T(8,128)(2,1)S(1)}, bf16[49,31]{0,1:T(8,128)(2,1)}, u32[]{:S(2)}) copy-start(bf16[49,31]{0,1:T(8,128)(2,1)} %param.11) | copy-start | bytes 9118
  0.6 1.0 %copy-start.1 = (f32[1,32,128]{2,1,0:T(8,128)S(1)}, f32[1,32,128]{2,1,0:T(8,128)}, u32[]{:S(2)}) copy-start(f32[1,32,128]{2,1,0:T(8,128)} %variance_ref.1) | copy-start | bytes 49156
  1.5 0.7 %copy-start = (f32[1,32,128]{2,1,0:T(8,128)S(1)}, f32[1,32,128]{2,1,0:T(8,128)}, u32[]{:S(2)}) copy-start(f32[1,32,128]{2,1,0:T(8,128)} %science_ref.1) | copy-start | bytes 49156
  1.5 0.7 %copy-start.2 = (bf16[2,128]{1,0:T(2,128)(2,1)S(1)}, bf16[2,128]{1,0:T(2,128)(2,1)}, u32[]{:S(2)}) copy-start(bf16[2,128]{1,0:T(2,128)(2,1)} %template_ref.1) | copy-start | bytes 1540
  1.5 0.7 %copy-start.3 = (s32[1,1,16]{2,1,0:T(1,128)S(1)}, s32[1,1,16]{2,1,0:T(1,128)}, u32[]{:S(2)}) copy-start(s32[1,1,16]{2,1,0:T(1,128)} %stamp_rows_ref.1) | copy-start | bytes 196
  1.5 0.7 %copy-start.4 = (s32[1,1,16]{2,1,0:T(1,128)S(1)}, s32[1,1,16]{2,1,0:T(1,128)}, u32[]{:S(2)}) copy-start(s32[1,1,16]{2,1,0:T(1,128)} %stamp_cols_ref.1) | copy-start | bytes 196
